TPU v7x, 128 devices: a whole 4x4x4 slice. The times are simulated.
128 devices in a mesh: member: 32 (over z, y_hi, x), tensor: 4 (over y_lo, core).
Axes of the slice: x: 4, y: 4 (y_hi: 2, y_lo: 2; y = y_hi * 2 + y_lo), z: 4, core: 2. Of those that a mesh axis runs over, the one named last changes fastest.
Arguments:
- series: float32 [16384], replicated, may hold values from -8 to 8
- starts: int32 [128], replicated, may hold values from 0 to 16216
- counts: int32 [32, 128], P(None, 'member'), may hold values from 0 to 3
- segment_lifting_matrix: float32 [32, 16, 2048], P('member', None, 'tensor')
- location_vector: float32 [32, 8, 2048], P('member', None, 'tensor'), may hold values from -8 to 8
- prelude_scaling_factor: float32 [32, 2048], P('member', 'tensor'), may hold values from 0.1 to 1.9
- expanding_matrix: bfloat16 [32, 2048, 8192], P('member', None, 'tensor'), may hold values from -0.125 to 0.125
- contracting_matrix: bfloat16 [32, 8192, 2048], P('member', 'tensor'), may hold values from -0.125 to 0.125
- final_scaling_factor: float32 [32, 2048], P('member', 'tensor'), may hold values from 0.1 to 1.9
- readout_matrix: bfloat16 [32, 8, 2048, 96], P('member', None, 'tensor'), may hold values from -0.1875 to 0.1875
Outputs:
- resampled_average_prediction: float32 [128, 96], P('member', 'tensor')
- error_percentiles: float32 [4, 96], P(None, 'tensor')
All inputs are finite; a program needn't handle non-finite values.
Results may differ from a plain program's by a relative error of at most 0.012.
Values may be sent and summed in bfloat16 or wider, within the bound.
No kernel may reach another device: no remote copies, remote signals or barrier semaphores. Data moves between devices by JAX's collectives and lax.ppermute only.
A program may use at most 128 MiB of HBM per device.

v0:
```python
import functools
import math

import jax
import jax.numpy as jnp
from jax import lax
from jax.experimental import pallas as pl
from jax.experimental.pallas import tpu as pltpu
from jax.sharding import PartitionSpec as P

BF, F32 = jnp.bfloat16, jnp.float32
PATCHES, PLEN, STRIDE, LOOK = 8, 16, 8, 72
WIN, D, SHARD, HIDDEN, HORIZONS = 128, 2048, 512, 2048, 96
KCAT = 256
MIB = 1 << 20
US = 10**9
GROUPS = ((0, 2), (2, 4), (4, 6), (6, 8))


def split3(x):
    a = x.astype(BF)
    rest = x - a.astype(F32)
    b = rest.astype(BF)
    c = (rest - b.astype(F32)).astype(BF)
    return a, b, c


def dot(a, b):
    return jnp.dot(a, b, preferred_element_type=F32)


def roll_left(x, by):
    lanes = x.shape[1]
    by = by % lanes
    return x if by == 0 else pltpu.roll(x, lanes - by, 1)


def shard_cols(t):
    return pl.ds(pl.multiple_of(SHARD * t, SHARD), SHARD)


def call(body, out_shape, in_specs, args, flops, nbytes, scratch=(), limit=24 * MIB, after=()):
    taken, held = len(in_specs), len(after)

    def run(*refs):
        body(*refs[:taken], *refs[taken + held :])

    args = tuple(
        pltpu.with_memory_space_constraint(x, pltpu.HBM if spec is HBM else pltpu.VMEM)
        for x, spec in zip(args, in_specs)
    ) + tuple(after)
    in_specs = list(in_specs) + [ANY] * held
    return pl.pallas_call(
        run,
        out_shape=out_shape,
        in_specs=in_specs,
        out_specs=jax.tree.map(lambda _: pl.BlockSpec(memory_space=pltpu.VMEM), out_shape),
        scratch_shapes=list(scratch),
        compiler_params=pltpu.CompilerParams(vmem_limit_bytes=limit),
        cost_estimate=pl.CostEstimate(flops=flops, bytes_accessed=nbytes, transcendentals=0),
    )(*args)


V = pl.BlockSpec(memory_space=pltpu.VMEM)
ANY = pl.BlockSpec(memory_space=pl.ANY)
HBM = pl.BlockSpec(memory_space=pltpu.HBM)


def pack_kernel(lifting, location, gain_one, gain_two, counts_h, down, packed, every, give, g1, g2, counts, scr, sem):
    t = lax.axis_index("tensor")
    loads = [
        pltpu.make_async_copy(lifting.at[0], packed.at[0:PLEN, :], sem.at[0]),
        pltpu.make_async_copy(location.at[0], packed.at[PLEN : PLEN + PATCHES, :], sem.at[1]),
        pltpu.make_async_copy(gain_one, g1, sem.at[2]),
        pltpu.make_async_copy(gain_two, g2, sem.at[3]),
        pltpu.make_async_copy(counts_h, counts, sem.at[4]),
        pltpu.make_async_copy(down.at[0, :, shard_cols(t ^ 3)], give, sem.at[5]),
    ]
    for load in loads:
        load.start()
    own, members = counts.shape
    scr[...] = jnp.zeros((WIN, WIN), F32)
    for load in loads[:5]:
        load.wait()
    row = lax.broadcasted_iota(jnp.int32, (8, SHARD), 0)
    packed[PLEN + PATCHES :, :] = jnp.where(row == 0, g1[...], jnp.where(row == 1, g2[...], 0.0))
    scr[:own, :members] = counts[...].astype(F32)
    columns = scr[...].T[:members]
    at = own * lax.axis_index("member")
    place = lax.broadcasted_iota(jnp.int32, (members, WIN), 1) - at
    placed = jnp.zeros((members, WIN), F32)
    for j in range(own):
        placed = jnp.where(place == j, columns[:, j : j + 1], placed)
    every[...] = placed
    loads[5].wait()


def lift_parts(t, shards, up, lhs):
    for n, (k, shard) in enumerate(shards):
        gain = shard[PLEN + PATCHES : PLEN + PATCHES + 1, :]
        row = lax.broadcasted_iota(jnp.int32, (32, SHARD), 0)
        rows = jnp.where(row < PLEN + PATCHES, shard[...] * gain, jnp.where(row == PLEN + PATCHES, gain, 0.0))
        for i, part in enumerate(split3(rows)):
            lhs[n, 32 * i : 32 * i + 32, :] = part
    for j in range(HIDDEN // 512):
        cols = slice(512 * j, 512 * j + 512)
        m = sum(dot(lhs[n], up[shard_cols(t ^ k), cols]) for n, (k, _) in enumerate(shards))
        yield cols, m[:32] + m[32:64] + m[64:96]


def windows_kernel(series_h, starts_h, down, give_y, q, info, target, series, starts, sem):
    t = lax.axis_index("tensor")
    small = [
        pltpu.make_async_copy(series_h, series, sem.at[0]),
        pltpu.make_async_copy(starts_h, starts, sem.at[1]),
    ]
    loads = [pltpu.make_async_copy(down.at[0, :, shard_cols(t ^ 1)], give_y, sem.at[2])]
    for load in small + loads:
        load.start()
    for load in small:
        load.wait()
    lane = lax.broadcasted_iota(jnp.int32, (WIN, WIN), 1)
    first = jnp.broadcast_to(starts[...].astype(F32), (WIN, WIN)).T.astype(jnp.int32)
    row, offset = first >> 7, first & 127
    picks = [(row + k == lane).astype(F32).astype(BF) for k in range(3)]
    parts = split3(series[...])
    rows = [sum(dot(pick, part) for part in parts) for pick in picks]
    x = jnp.concatenate(rows, axis=1)
    offset = jnp.concatenate([offset] * 3, axis=1)
    for bit in range(7):
        x = jnp.where((offset >> bit) & 1 == 1, roll_left(x, 1 << bit), x)
    target[...] = roll_left(x, LOOK)[:, :WIN].T
    look = x[:, :WIN]
    center = jnp.sum(jnp.where(lane < LOOK, look, 0.0), axis=1, keepdims=True) * (1.0 / LOOK)
    dev = jnp.where(lane < LOOK, look - center, 0.0)
    spread = jnp.sqrt(jnp.sum(dev * dev, axis=1, keepdims=True) * (1.0 / LOOK) + 1e-05)
    normed = dev / spread
    pair = jnp.where(lane == 0, center, jnp.where(lane == 1, spread, 0.0)).T
    info[...] = pair[:8]
    block = lane // 32
    for p in range(PATCHES):
        one = jnp.where(lane < PLEN, roll_left(normed, STRIDE * p), 0.0)
        one = jnp.where(lane == PLEN + p, 1.0, one)
        two = one + pltpu.roll(one, 32, 1)
        four = two + pltpu.roll(two, 64, 1)
        a, b, c = (v.astype(F32) for v in split3(four))
        q[p, :, :WIN] = jnp.where(block < 2, a, b).astype(BF)
        q[p, :, WIN:] = jnp.where(block == 0, a, jnp.where(block == 1, c, 0.0)).astype(BF)
    for load in loads:
        load.wait()


def cat_rows(x):
    b1, b2, b3 = split3(x)
    zero = jnp.zeros_like(b1)
    return [b1, b2, b1, b2, b3, b1, zero, zero]


def lift_kernel(up, s0, s1, s2, s3, mine, late, m24, ecat, every, lhs):
    t = lax.axis_index("tensor")
    every[...] = mine[...] + late[...]
    shards = (s0, s1, s2, s3)
    mean = sum(jnp.sum(s[...], axis=1, keepdims=True) for s in shards) * (1.0 / D)
    keep = lax.broadcasted_iota(jnp.int32, (32, SHARD), 0) < PLEN + PATCHES
    for cols, m in lift_parts(t, tuple(enumerate(shards)), up, lhs):
        m24[:, cols] = m - mean * m[PLEN + PATCHES : PLEN + PATCHES + 1, :]
    for k, shard in enumerate(shards):
        centred = jnp.where(keep, shard[...] - mean, 0.0)
        for i, part in enumerate(cat_rows(centred)):
            ecat[k, 32 * i : 32 * i + 32, :] = part


def spread_rows(m24, mcat):
    for j in range(HIDDEN // 512):
        cols = slice(512 * j, 512 * j + 512)
        row = lax.broadcasted_iota(jnp.int32, (32, 512), 0)
        for i, part in enumerate(cat_rows(jnp.where(row < PLEN + PATCHES, m24[:, cols], 0.0))):
            mcat[32 * i : 32 * i + 32, cols] = part


def scale_kernel(q, ecat, m24, rstd, mcat):
    spread_rows(m24, mcat)
    for p in range(0, PATCHES, 2):
        square = jnp.zeros((2 * WIN, 128), F32)
        for k in range(4):
            dev = dot(q[p : p + 2].reshape(2 * WIN, KCAT), ecat[k])
            for c in range(SHARD // 128):
                piece = dev[:, 128 * c : 128 * c + 128]
                square = square + piece * piece
        var = jnp.sum(square, axis=1, keepdims=True) * (1.0 / D)
        rstd[p : p + 2] = jnp.broadcast_to(lax.rsqrt(var + 1e-05), (2 * WIN, 128)).reshape(2, WIN, 128)


def gelu(h):
    c = math.sqrt(2.0 / math.pi)
    half = 0.5 * h
    return half + half * jnp.tanh(h * (c + (c * 0.044715) * (h * h)))


def away_body(group, q, rstd, mcats, downs, act, send):
    rows = (group[1] - group[0]) * WIN
    x = q[group[0] : group[1]].reshape(rows, KCAT)
    scale = rstd[group[0] : group[1]].reshape(rows, 128)[:, :1]
    downs = (downs[0][:, shard_cols(lax.axis_index("tensor") ^ 2)], downs[1][...])
    for side in range(2):
        for j in range(HIDDEN // 512):
            cols = slice(512 * j, 512 * j + 512)
            at = slice(HIDDEN * side + 512 * j, HIDDEN * side + 512 * (j + 1))
            act[:, at] = gelu(dot(x, mcats[side][:, cols]) * scale).astype(BF)
    send[...] = (dot(act[:, :HIDDEN], downs[0]) + dot(act[:, HIDDEN:], downs[1])).astype(BF)


def first_away_kernel(q, rstd, m_own, m24_peer, down, d_peer, m_peer, act, send):
    spread_rows(m24_peer, m_peer)
    away_body(GROUPS[0], q, rstd, (m_own, m_peer), (down, d_peer), act, send)


def away_kernel(group, q, rstd, m_own, m_peer, down, d_peer, act, send):
    away_body(group, q, rstd, (m_own, m_peer), (down, d_peer), act, send)


def add_stats(table, p, x):
    lane = lax.broadcasted_iota(jnp.int32, (WIN, WIN), 1)
    mean = jnp.sum(x, axis=1, keepdims=True) * (1.0 / SHARD)
    off = x - mean
    square = jnp.sum(off * off, axis=1, keepdims=True)
    return jnp.where(lane == p, mean, jnp.where(lane == PATCHES + p, square, table))


def home_rows(group, q, ecat, down, d_peer, act):
    own = down[:, shard_cols(lax.axis_index("tensor"))]
    x = dot(act[:, :HIDDEN], own) + dot(act[:, HIDDEN:], d_peer[...])
    return x + dot(q[group[0] : group[1]].reshape((group[1] - group[0]) * WIN, KCAT), ecat[0])


def home_kernel(q, ecat, d_own, d_peer, a0, a1, part):
    for group, act in zip(GROUPS[:2], (a0, a1)):
        part[WIN * group[0] : WIN * group[1], :] = home_rows(group, q, ecat, d_own, d_peer, act)


def weights(info, counts, members, own):
    slot = lax.axis_index("member")
    share = 1.0 / (1.0 + counts)
    member = lax.broadcasted_iota(jnp.int32, (members, WIN), 0)
    lane = lax.broadcasted_iota(jnp.int32, (1, WIN), 1)
    factor = info[1:2, :] / jnp.sum(share, axis=0, keepdims=True)
    if members > 4:
        factor = jnp.where((((lane // own) ^ slot) >> 2) & 1 == 0, factor, 0.0)
    rows = [jnp.sum(jnp.where(member == slot ^ k, share, 0.0), axis=0, keepdims=True) * factor for k in (0, 4)]
    row = lax.broadcasted_iota(jnp.int32, (8, WIN), 0)
    return jnp.where(row == 0, rows[0], jnp.where(row == 1, rows[1], 0.0))


def state_kernel(
    members, own, q, ecat, d_own, d_peer, a2, a3, part, c0, c1, c2, info, mine, late, state, last, stats, shares
):
    shares[...] = weights(info, mine[...] + late[...], members, own)
    last[...] = home_rows(GROUPS[3], q, ecat, d_own, d_peer, a3)
    table = jnp.zeros((WIN, WIN), F32)
    for g, cross in enumerate((c0, c1, c2)):
        group = GROUPS[g]
        rows = slice(WIN * group[0], WIN * group[1])
        x = part[rows, :] if g < 2 else home_rows(group, q, ecat, d_own, d_peer, a2)
        x = x + cross[...].astype(F32)
        state[rows, :] = x
        for i, p in enumerate(range(*group)):
            table = add_stats(table, p, x[i * WIN : (i + 1) * WIN])
    stats[...] = table.T[: 2 * PATCHES]


def last_state_kernel(last, cross, prev, state, stats):
    x = last[...] + cross[...].astype(F32)
    state[...] = x
    table = jnp.zeros((WIN, WIN), F32)
    for i, p in enumerate(range(*GROUPS[3])):
        table = add_stats(table, p, x[i * WIN : (i + 1) * WIN])
    stats[...] = prev[...] + table.T[: 2 * PATCHES]


def head_kernel(stats, state, last, heads, shard, shares, send, keep, scr):
    core = lax.axis_index("tensor") & 1
    first = GROUPS[3][0]
    scale = lax.rsqrt(stats[PATCHES:, :] * (1.0 / D) + 1e-05)
    table = jnp.concatenate([stats[:PATCHES, :], scale, jnp.zeros((WIN - 2 * PATCHES, WIN), F32)], axis=0).T
    total = jnp.zeros((WIN, HORIZONS), F32)
    for p in range(PATCHES):
        x = state[p * WIN : (p + 1) * WIN, :] if p < first else last[(p - first) * WIN : (p - first + 1) * WIN, :]
        y = (x - table[:, p : p + 1]) * table[:, PATCHES + p : PATCHES + p + 1] * shard[25:26, :]
        total = total + lax.dot_general(
            y.astype(BF), heads[p], (((1,), (1,)), ((), ())), preferred_element_type=F32
        )
    scr[:, :HORIZONS] = total
    scr[:, HORIZONS:] = jnp.zeros((WIN, WIN - HORIZONS), F32)
    scr[...] = scr[...].T
    for c in range(2):
        for out, side in ((keep, core), (send, 1 - core)):
            out[24 * c : 24 * c + 24, :] = scr[pl.ds(pl.multiple_of(48 * c + 24 * side, 8), 24), :]
    keep[48:, :] = 0.5 * shares[...]
    send[48:, :] = jnp.zeros((8, WIN), F32)


def weigh_kernel(mine, theirs, out):
    at = pl.ds(pl.multiple_of(24 * (lax.axis_index("tensor") >> 1), 8), 24)
    here = mine[48:49, :] + theirs[49:50, :]
    there = mine[49:50, :] + theirs[48:49, :]
    out[...] = mine[at, :] * here + theirs[at, :] * there


def rank_kernel(levels, own, total, info, target, average, levels_out, scr, res, ranks):
    t = lax.axis_index("tensor")
    slot = lax.axis_index("member")
    per = total.shape[0]
    pred = total[...] + info[0:1, :]
    wanted = target[pl.ds(pl.multiple_of(24 * t, 8), per), :]
    resid = jnp.abs(wanted - pred)
    scr[...] = jnp.zeros((WIN, WIN), F32)
    scr[:per, :] = pred
    scr[...] = scr[...].T
    if own % 8 == 0:
        average[...] = scr[pl.ds(pl.multiple_of(own * slot, 8), own), :per]
    else:
        at = own * slot
        rows = scr[pl.ds(pl.multiple_of((at // 8) * 8, 8), 8), :per]
        pick = rows[:own]
        for s in range(1, 8 // own):
            pick = jnp.where(at % 8 == s * own, rows[s * own : (s + 1) * own], pick)
        average[...] = pick
    res[...] = jnp.zeros((WIN, WIN), F32)
    res[:per, :] = resid
    across = res[...].T
    j = lax.broadcasted_iota(jnp.int32, (WIN, WIN), 0)
    i = lax.broadcasted_iota(jnp.int32, (WIN, WIN), 1)
    earlier = j < i
    for h in range(per):
        row, col = resid[h : h + 1, :], across[:, h : h + 1]
        before = (col < row) | ((col == row) & earlier)
        ranks[h : h + 1, :] = jnp.sum(before.astype(F32), axis=0, keepdims=True)
    order = ranks[...]
    lane = lax.broadcasted_iota(jnp.int32, (per, WIN), 1)
    table = jnp.zeros((per, WIN), F32)
    for n, level in enumerate(levels):
        value = jnp.sum(jnp.where(order == float(level), resid, 0.0), axis=1, keepdims=True)
        table = jnp.where(lane == n, value, table)
    res[:per, :] = table
    levels_out[...] = res[...].T[: len(levels), :per]


def per_device(series, starts, counts, lifting, location, gain_one, up, down, gain_two, readout):
    members = lax.axis_size("member")
    own = counts.shape[1]
    sds = jax.ShapeDtypeStruct

    def over_tensor(x, k):
        return lax.ppermute(x, "tensor", [(i, i ^ k) for i in range(4)])

    def over_member(x, k):
        return lax.ppermute(x, "member", [(i, i ^ k) for i in range(members)])

    shard_bf = pltpu.VMEM((D, SHARD), BF)
    packed, every, give_x = call(
        pack_kernel,
        (pltpu.VMEM((32, SHARD), F32), pltpu.VMEM((members, WIN), F32), shard_bf),
        [HBM] * 6,
        (lifting, location, gain_one, gain_two, counts.T, down),
        2 * US,
        1000,
        [
            pltpu.VMEM((1, SHARD), F32),
            pltpu.VMEM((1, SHARD), F32),
            pltpu.VMEM((own, members), jnp.int32),
            pltpu.VMEM((WIN, WIN), F32),
            pltpu.SemaphoreType.DMA((6,)),
        ],
    )
    shards = [packed] + [over_tensor(packed, k) for k in (1, 2, 3)]
    peer_x = over_tensor(give_x, 1)

    heads = jnp.swapaxes(readout[0], 1, 2)
    up = up[0]
    give_y, q, info, target = call(
        windows_kernel,
        (
            shard_bf,
            pltpu.VMEM((PATCHES, WIN, KCAT), BF),
            pltpu.VMEM((8, WIN), F32),
            pltpu.VMEM((WIN, WIN), F32),
        ),
        [HBM] * 3,
        (series.reshape(WIN, WIN), starts.reshape(1, WIN), down),
        5 * US,
        1000,
        [pltpu.VMEM((WIN, WIN), F32), pltpu.VMEM((1, WIN), jnp.int32), pltpu.SemaphoreType.DMA((3,))],
        after=(packed,),
    )

    hops = [k for k in (1, 3, 8, 24) if k < members]
    steps = iter(hops)

    def hop(value, after=None):
        k = next(steps, None)
        if after is not None:
            value = lax.optimization_barrier((value, after))[0]
        return value if k is None else value + over_member(value, k)

    def hop_parts(value, after=None):
        k = next(steps, None)
        if after is not None:
            value = lax.optimization_barrier((value, after))[0]
        return value, jnp.zeros_like(value) if k is None else over_member(value, k)

    every, late = hop_parts(every)
    m24, ecat, every = call(
        lift_kernel,
        (pltpu.VMEM((32, HIDDEN), F32), pltpu.VMEM((4, KCAT, SHARD), BF), pltpu.VMEM((members, WIN), F32)),
        [V] * 7,
        (up, *shards, every, late),
        3 * US,
        1000,
        [pltpu.VMEM((4, 96, SHARD), BF)],
        after=(info,),
    )
    m24_peer = over_tensor(m24, 1)
    mcat_shape = pltpu.VMEM((KCAT, HIDDEN), BF)
    rstd, m_own = call(
        scale_kernel,
        (pltpu.VMEM((PATCHES, WIN, 128), F32), mcat_shape),
        [V] * 3,
        (q, ecat, m24),
        2 * US,
        1000,
    )

    def sums(group):
        rows = (group[1] - group[0]) * WIN
        return pltpu.VMEM((rows, 2 * HIDDEN), BF), pltpu.VMEM((rows, SHARD), BF)

    m_peer, act, send = call(
        first_away_kernel,
        (mcat_shape, *sums(GROUPS[0])),
        [V] * 6,
        (q, rstd, m_own, m24_peer, down[0], peer_x),
        4 * US,
        1000,
    )
    acts, crossed = [act], [over_tensor(send, 2)]
    fed = (q, rstd, m_own, m_peer, down[0], peer_x)
    peer_y = over_tensor(lax.optimization_barrier((give_y, send))[0], 1)
    for g in range(1, 4):
        act, send = call(
            functools.partial(away_kernel, GROUPS[g]),
            sums(GROUPS[g]),
            [V] * 6,
            fed,
            4 * US,
            1000,
            after=(every, crossed[g - 2]) if g > 1 else (),
        )
        acts.append(act)
        crossed.append(over_tensor(send, 2))
        if g < 3:
            every = hop(every, send)
    every, late = hop_parts(every, send)
    homes = (q, ecat, down[0], peer_y)
    (part,) = call(
        home_kernel,
        (pltpu.VMEM((GROUPS[1][1] * WIN, SHARD), F32),),
        [V] * 6,
        (*homes, *acts[:2]),
        US // 10,
        1000,
        after=(send,),
    )
    tail = (GROUPS[3][1] - GROUPS[3][0]) * WIN
    state, last, stats, shares = call(
        functools.partial(state_kernel, members, own),
        (
            pltpu.VMEM((GROUPS[2][1] * WIN, SHARD), F32),
            pltpu.VMEM((tail, SHARD), F32),
            pltpu.VMEM((2 * PATCHES, WIN), F32),
            pltpu.VMEM((8, WIN), F32),
        ),
        [V] * 13,
        (*homes, *acts[2:], part, *crossed[:3], info, every, late),
        5 * US,
        1000,
    )
    last, stats = call(
        last_state_kernel,
        (pltpu.VMEM((tail, SHARD), F32), pltpu.VMEM((2 * PATCHES, WIN), F32)),
        [V] * 3,
        (last, crossed[3], stats),
        US,
        1000,
    )
    features = SHARD
    for k in (1, 2):
        other = over_tensor(stats, k)
        gap = stats[:PATCHES] - other[:PATCHES]
        square = stats[PATCHES:] + other[PATCHES:] + (0.5 * features) * (gap * gap)
        stats = jnp.concatenate([0.5 * (stats[:PATCHES] + other[:PATCHES]), square], axis=0)
        features *= 2
    sent, held = call(
        head_kernel,
        (pltpu.VMEM((56, WIN), F32),) * 2,
        [V] * 6,
        (stats, state, last, heads, packed, shares),
        US,
        1000,
        [pltpu.VMEM((WIN, WIN), F32)],
    )
    total = held + over_tensor(sent, 1)
    total = total + over_tensor(total, 2)
    if members > 4:
        pairs = [(4 * m + t, 4 * (m ^ 4) + (t ^ 2)) for m in range(members) for t in range(4)]
        met = lax.ppermute(total, ("member", "tensor"), pairs)
    else:
        met = jnp.zeros_like(total)
    (total,) = call(weigh_kernel, (pltpu.VMEM((24, WIN), F32),), [V] * 2, (total, met), US, 1000)
    for ring in ((1, 2, 3), (8, 16, 24)):
        if ring[-1] < members:
            got = [over_member(total, k) for k in ring]
            total = total + got[0] + got[1] + got[2]

    levels = tuple(WIN * n // 100 for n in (50, 80, 90, 95))
    return call(
        functools.partial(rank_kernel, levels, own),
        (sds((own, 24), F32), sds((4, 24), F32)),
        [V] * 3,
        (total, info, target),
        US,
        1000,
        [pltpu.VMEM((WIN, WIN), F32), pltpu.VMEM((WIN, WIN), F32), pltpu.VMEM((24, WIN), F32)],
    )


def solution(mesh):
    placed = (
        P(),
        P(),
        P(None, "member"),
        P("member", None, "tensor"),
        P("member", None, "tensor"),
        P("member", "tensor"),
        P("member", None, "tensor"),
        P("member", "tensor", None),
        P("member", "tensor"),
        P("member", None, "tensor", None),
    )
    return jax.shard_map(
        per_device,
        mesh=mesh,
        in_specs=placed,
        out_specs=(P("member", "tensor"), P(None, "tensor")),
        check_vma=False,
    )
```

profile of v0, /device:TPU:0, one launch (start us, length us, event | category | flops | bytes accessed | tf_op | source)
XLA Modules:
  0.0 76.8 jit_solution(3652710004469270430)
XLA Ops:
  0.6 1.9 %shard_map.113 = (f32[32,512]{1,0:T(8,128)S(1)}, f32[32,128]{1,0:T(8,128)S(1)}, bf16[2048,512]{1,0:T(8,128)(2,1)S(1)}) custom-call(f32[1,16,512]{2,1,0:T(8,128)} %refs_0_.1, f32[1,8,512]{2,1,0:T(8,128)} %refs_1_.1, f32[1,512]{1,0:T(1,128)} %refs_2_.2, f32[1,512]{1,0:T(1,128)} %refs_3_.1, s32[4,32]{1,0:T(4,128)} %bitcast.20, bf16[1,2048,2048]{2,1,0:T(8,128)(2,1)} %refs_2_.3), custom_call_target="tpu_custom_call" | custom-call | flops 2000000000 | bytes 1000 | tf_op jit(solution)/shard_map/pallas_call | solution.py:53
  2.6 1.8 %collective-permute-start.2 = (f32[32,512]{1,0:T(8,128)S(1)}, f32[32,512]{1,0:T(8,128)S(1)}, u32[]{:S(2)}, u32[]{:S(2)}) collective-permute-start(f32[32,512]{1,0:T(8,128)S(1)} %get-tuple-element.35.refs_3_.refs_1_.refs_4_), channel_id=1, source_target_pairs={{0,3},{1,2},{2,1},{3,0},{4,7},{5,6},{6,5},{7,4},{8,11},{9,10},{10,... | collective-permute-start | bytes 196616 | tf_op jit(solution)/shard_map/ppermute | solution.py:354
  4.8 1.6 %collective-permute-start.3 = (f32[32,128]{1,0:T(8,128)S(1)}, f32[32,128]{1,0:T(8,128)S(1)}, u32[]{:S(2)}, u32[]{:S(2)}) collective-permute-start(f32[32,128]{1,0:T(8,128)S(1)} %get-tuple-element.37.refs_5_), channel_id=1, source_target_pairs={{0,4},{4,0},{8,12},{12,8},{16,20},{20,16},{24,28},{28,24},{32,36},... | collective-permute-start | bytes 49160 | tf_op jit(solution)/shard_map/ppermute | solution.py:357
  6.4 2.7 %shard_map.114 = (bf16[2048,512]{1,0:T(8,128)(2,1)S(1)}, bf16[8,128,256]{2,1,0:T(8,128)(2,1)S(1)}, f32[8,128]{1,0:T(8,128)S(1)}, f32[128,128]{1,0:T(8,128)S(1)}) custom-call(f32[128,128]{1,0:T(8,128)} %bitcast.21, s32[1,128]{1,0:T(1,128)} %bitcast.22, bf16[1,2048,2048]{2,1,0:T(8,128)(2,1)} %refs_2_.3, f32[32,512]{1,0:T(8,128)S(1)} %get-tuple-element.35.refs_3_.refs_1_.refs_4_), custom_call_target="tpu_custom_call" | custom-call | flops 5000000000 | bytes 1000 | tf_op jit(solution)/shard_map/pallas_call | solution.py:53
  9.2 1.5 %shard_map.115 = (f32[32,2048]{1,0:T(8,128)S(1)}, bf16[4,256,512]{2,1,0:T(8,128)(2,1)S(1)}, f32[32,128]{1,0:T(8,128)S(1)}) custom-call(bf16[2048,2048]{1,0:T(8,128)(2,1)S(1)} %bitcast.18, f32[32,512]{1,0:T(8,128)S(1)} %get-tuple-element.35.refs_3_.refs_1_.refs_4_, f32[32,512]{1,0:T(8,128)S(1)} %collective-permute-done.refs_2_, ...), custom_call_target="tpu_custom_call" | custom-call | flops 3000000000 | bytes 1000 | tf_op jit(solution)/shard_map/pallas_call | solution.py:53
  12.5 2.8 %shard_map.117 = (bf16[256,2048]{1,0:T(8,128)(2,1)S(1)}, bf16[256,4096]{1,0:T(8,128)(2,1)S(1)}, bf16[256,512]{1,0:T(8,128)(2,1)S(1)}) custom-call(bf16[8,128,256]{2,1,0:T(8,128)(2,1)S(1)} %get-tuple-element.36.refs_0_, f32[8,128,128]{2,1,0:T(8,128)S(1)} %get-tuple-element.42.refs_1_, bf16[256,2048]{1,0:T(8,128)(2,1)S(1)} %get-tuple-element.43.refs_2_, ...), custom_call_target="tpu_custom_call" | custom-call | flops 4000000000 | bytes 1000 | tf_op jit(solution)/shard_map/pallas_call | solution.py:53
  15.7 1.6 %collective-permute-start.8 = (bf16[256,512]{1,0:T(8,128)(2,1)S(1)}, bf16[256,512]{1,0:T(8,128)(2,1)S(1)}, u32[]{:S(2)}, u32[]{:S(2)}) collective-permute-start(bf16[256,512]{1,0:T(8,128)(2,1)S(1)} %get-tuple-element.45), channel_id=1, source_target_pairs={{0,2},{1,3},{2,0},{3,1},{4,6},{5,7},{6,4},{7,5},{8,10},{9,11},{10,... | collective-permute-start | bytes 786440 | tf_op jit(solution)/shard_map/ppermute | solution.py:354
  17.3 2.8 %shard_map.118 = (bf16[256,4096]{1,0:T(8,128)(2,1)S(1)}, bf16[256,512]{1,0:T(8,128)(2,1)S(1)}) custom-call(bf16[8,128,256]{2,1,0:T(8,128)(2,1)S(1)} %get-tuple-element.36.refs_0_, f32[8,128,128]{2,1,0:T(8,128)S(1)} %get-tuple-element.42.refs_1_, bf16[256,2048]{1,0:T(8,128)(2,1)S(1)} %get-tuple-element.43.refs_2_, ...), custom_call_target="tpu_custom_call" | custom-call | flops 4000000000 | bytes 1000 | tf_op jit(solution)/shard_map/pallas_call | solution.py:53
  20.1 2.3 %collective-permute-start.7 = (f32[32,128]{1,0:T(8,128)S(1)}, f32[32,128]{1,0:T(8,128)S(1)}, u32[]{:S(2)}, u32[]{:S(2)}) collective-permute-start(f32[32,128]{1,0:T(8,128)S(1)} %get-tuple-element.50), channel_id=1, source_target_pairs={{0,12},{4,8},{8,4},{12,0},{16,28},{20,24},{24,20},{28,16},{32,44},... | collective-permute-start | bytes 49160 | tf_op jit(solution)/shard_map/ppermute | solution.py:357
  22.8 2.3 %collective-permute-done.7 = f32[32,128]{1,0:T(8,128)S(1)} collective-permute-done((f32[32,128]{1,0:T(8,128)S(1)}, f32[32,128]{1,0:T(8,128)S(1)}, u32[]{:S(2)}, u32[]{:S(2)}) %collective-permute-start.7) | collective-permute-done | bytes 16416 | tf_op jit(solution)/shard_map/ppermute | solution.py:357
  25.1 2.8 %shard_map.119 = (bf16[256,4096]{1,0:T(8,128)(2,1)S(1)}, bf16[256,512]{1,0:T(8,128)(2,1)S(1)}) custom-call(bf16[8,128,256]{2,1,0:T(8,128)(2,1)S(1)} %get-tuple-element.36.refs_0_, f32[8,128,128]{2,1,0:T(8,128)S(1)} %get-tuple-element.42.refs_1_, bf16[256,2048]{1,0:T(8,128)(2,1)S(1)} %get-tuple-element.43.refs_2_, ...), custom_call_target="tpu_custom_call" | custom-call | flops 4000000000 | bytes 1000 | tf_op jit(solution)/shard_map/pallas_call | solution.py:53
  27.9 2.0 %collective-permute-start.9 = (f32[32,128]{1,0:T(8,128)S(1)}, f32[32,128]{1,0:T(8,128)S(1)}, u32[]{:S(2)}, u32[]{:S(2)}) collective-permute-start(f32[32,128]{1,0:T(8,128)S(1)} %add.48.refs_6_), channel_id=1, source_target_pairs={{0,32},{4,36},{8,40},{12,44},{16,48},{20,52},{24,56},{28,60},{32,0... | collective-permute-start | bytes 49160 | tf_op jit(solution)/shard_map/ppermute | solution.py:357
  31.7 2.8 %shard_map.120 = (bf16[256,4096]{1,0:T(8,128)(2,1)S(1)}, bf16[256,512]{1,0:T(8,128)(2,1)S(1)}) custom-call(bf16[8,128,256]{2,1,0:T(8,128)(2,1)S(1)} %get-tuple-element.36.refs_0_, f32[8,128,128]{2,1,0:T(8,128)S(1)} %get-tuple-element.42.refs_1_, bf16[256,2048]{1,0:T(8,128)(2,1)S(1)} %get-tuple-element.43.refs_2_, ...), custom_call_target="tpu_custom_call" | custom-call | flops 4000000000 | bytes 1000 | tf_op jit(solution)/shard_map/pallas_call | solution.py:53
  34.5 4.1 %collective-permute-start.12 = (f32[32,128]{1,0:T(8,128)S(1)}, f32[32,128]{1,0:T(8,128)S(1)}, u32[]{:S(2)}, u32[]{:S(2)}) collective-permute-start(f32[32,128]{1,0:T(8,128)S(1)} %add.49.refs_6_.refs_11_), channel_id=1, source_target_pairs={{0,96},{4,100},{8,104},{12,108},{16,112},{20,116},{24,120},{28,124... | collective-permute-start | bytes 49160 | tf_op jit(solution)/shard_map/ppermute | solution.py:357
  39.9 2.5 %shard_map.121.refs_6_ = f32[512,512]{1,0:T(8,128)S(1)} custom-call(bf16[8,128,256]{2,1,0:T(8,128)(2,1)S(1)} %get-tuple-element.36.refs_0_, bf16[4,256,512]{2,1,0:T(8,128)(2,1)S(1)} %get-tuple-element.39.refs_1_, bf16[2048,2048]{1,0:T(8,128)(2,1)S(1)} %bitcast.14, bf16[2048,512]{1,0:T(8,128)(2,1)S(1)} %collective-permute-done.6.refs_3_, ...), custom_call_target="tpu_custom_call" | custom-call | flops 100000000 | bytes 1000 | tf_op jit(solution)/shard_map/pallas_call | solution.py:53
  42.4 2.8 %shard_map.122 = (f32[768,512]{1,0:T(8,128)S(1)}, f32[256,512]{1,0:T(8,128)S(1)}, f32[16,128]{1,0:T(8,128)S(1)}, f32[8,128]{1,0:T(8,128)S(1)}) custom-call(bf16[8,128,256]{2,1,0:T(8,128)(2,1)S(1)} %get-tuple-element.36.refs_0_, bf16[4,256,512]{2,1,0:T(8,128)(2,1)S(1)} %get-tuple-element.39.refs_1_, bf16[2048,2048]{1,0:T(8,128)(2,1)S(1)} %bitcast.15, ...), custom_call_target="tpu_custom_call" | custom-call | flops 5000000000 | bytes 1000 | tf_op jit(solution)/shard_map/pallas_call | solution.py:53
  47.9 2.5 %collective-permute-done.15 = f32[16,128]{1,0:T(8,128)S(1)} collective-permute-done((f32[16,128]{1,0:T(8,128)S(1)}, f32[16,128]{1,0:T(8,128)S(1)}, u32[]{:S(2)}, u32[]{:S(2)}) %collective-permute-start.15) | collective-permute-done | bytes 8224 | tf_op jit(solution)/shard_map/ppermute | solution.py:354
  53.7 2.8 %collective-permute-done.17 = f32[56,128]{1,0:T(8,128)S(1)} collective-permute-done((f32[56,128]{1,0:T(8,128)S(1)}, f32[56,128]{1,0:T(8,128)S(1)}, u32[]{:S(2)}, u32[]{:S(2)}) %collective-permute-start.17) | collective-permute-done | bytes 28704 | tf_op jit(solution)/shard_map/ppermute | solution.py:354
  56.5 2.2 %collective-permute-start.18 = (f32[56,128]{1,0:T(8,128)S(1)}, f32[56,128]{1,0:T(8,128)S(1)}, u32[]{:S(2)}, u32[]{:S(2)}) collective-permute-start(f32[56,128]{1,0:T(8,128)S(1)} %add.57.refs_0_), channel_id=1, source_target_pairs={{0,18},{1,19},{2,16},{3,17},{4,22},{5,23},{6,20},{7,21},{8,26},{9,... | collective-permute-start | bytes 86024 | tf_op jit(solution)/shard_map/ppermute | solution.py:515
  58.7 2.8 %collective-permute-done.18.refs_1_ = f32[56,128]{1,0:T(8,128)S(1)} collective-permute-done((f32[56,128]{1,0:T(8,128)S(1)}, f32[56,128]{1,0:T(8,128)S(1)}, u32[]{:S(2)}, u32[]{:S(2)}) %collective-permute-start.18) | collective-permute-done | bytes 28704 | tf_op jit(solution)/shard_map/ppermute | solution.py:515
  61.6 2.2 %collective-permute-start.21 = (f32[24,128]{1,0:T(8,128)S(1)}, f32[24,128]{1,0:T(8,128)S(1)}, u32[]{:S(2)}, u32[]{:S(2)}) collective-permute-start(f32[24,128]{1,0:T(8,128)S(1)} %shard_map.125), channel_id=1, source_target_pairs={{0,12},{4,8},{8,4},{12,0},{16,28},{20,24},{24,20},{28,16},{32,44},... | collective-permute-start | bytes 36872 | tf_op jit(solution)/shard_map/ppermute | solution.py:357
  66.5 2.5 %collective-permute-done.20 = f32[24,128]{1,0:T(8,128)S(1)} collective-permute-done((f32[24,128]{1,0:T(8,128)S(1)}, f32[24,128]{1,0:T(8,128)S(1)}, u32[]{:S(2)}, u32[]{:S(2)}) %collective-permute-start.20) | collective-permute-done | bytes 12320 | tf_op jit(solution)/shard_map/ppermute | solution.py:357
  70.9 2.2 %collective-permute-start.22 = (f32[24,128]{1,0:T(8,128)S(1)}, f32[24,128]{1,0:T(8,128)S(1)}, u32[]{:S(2)}, u32[]{:S(2)}) collective-permute-start(f32[24,128]{1,0:T(8,128)S(1)} %add_add_fusion.1), channel_id=1, source_target_pairs={{0,32},{4,36},{8,40},{12,44},{16,48},{20,52},{24,56},{28,60},{32,0... | collective-permute-start | bytes 36872 | tf_op jit(solution)/shard_map/ppermute | solution.py:357
  74.0 1.4 %collective-permute-done.23 = f32[24,128]{1,0:T(8,128)S(1)} collective-permute-done((f32[24,128]{1,0:T(8,128)S(1)}, f32[24,128]{1,0:T(8,128)S(1)}, u32[]{:S(2)}, u32[]{:S(2)}) %collective-permute-start.23) | collective-permute-done | bytes 12320 | tf_op jit(solution)/shard_map/ppermute | solution.py:357
  (62 shorter events, 19.1 us)
Async XLA Ops:
  2.5 9.9 %collective-permute-start.5 = (bf16[2048,512]{1,0:T(8,128)(2,1)S(1)}, bf16[2048,512]{1,0:T(8,128)(2,1)S(1)}, u32[]{:S(2)}, u32[]{:S(2)}) collective-permute-start(bf16[2048,512]{1,0:T(8,128)(2,1)S(1)} %get-tuple-element.44), channel_id=1, source_target_pairs={{0,1},{1,0},{2,3},{3,2},{4,5},{5,4},{6,7},{7,6},{8,9},{9,8},{10,11... | collective-permute-start | bytes 6291464 | tf_op jit(solution)/shard_map/ppermute | solution.py:354
  2.6 6.5 %collective-permute-start.2 = (f32[32,512]{1,0:T(8,128)S(1)}, f32[32,512]{1,0:T(8,128)S(1)}, u32[]{:S(2)}, u32[]{:S(2)}) collective-permute-start(f32[32,512]{1,0:T(8,128)S(1)} %get-tuple-element.35.refs_3_.refs_1_.refs_4_), channel_id=1, source_target_pairs={{0,3},{1,2},{2,1},{3,0},{4,7},{5,6},{6,5},{7,4},{8,11},{9,10},{10,... | collective-permute-start | bytes 196616 | tf_op jit(solution)/shard_map/ppermute | solution.py:354
  4.4 4.7 %collective-permute-start.1 = (f32[32,512]{1,0:T(8,128)S(1)}, f32[32,512]{1,0:T(8,128)S(1)}, u32[]{:S(2)}, u32[]{:S(2)}) collective-permute-start(f32[32,512]{1,0:T(8,128)S(1)} %get-tuple-element.35.refs_3_.refs_1_.refs_4_), channel_id=1, source_target_pairs={{0,2},{1,3},{2,0},{3,1},{4,6},{5,7},{6,4},{7,5},{8,10},{9,11},{10,... | collective-permute-start | bytes 196616 | tf_op jit(solution)/shard_map/ppermute | solution.py:354
  4.8 4.4 %collective-permute-start = (f32[32,512]{1,0:T(8,128)S(1)}, f32[32,512]{1,0:T(8,128)S(1)}, u32[]{:S(2)}, u32[]{:S(2)}) collective-permute-start(f32[32,512]{1,0:T(8,128)S(1)} %get-tuple-element.35.refs_3_.refs_1_.refs_4_), channel_id=1, source_target_pairs={{0,1},{1,0},{2,3},{3,2},{4,5},{5,4},{6,7},{7,6},{8,9},{9,8},{10,11... | collective-permute-start | bytes 196616 | tf_op jit(solution)/shard_map/ppermute | solution.py:354
  4.8 4.3 %collective-permute-start.3 = (f32[32,128]{1,0:T(8,128)S(1)}, f32[32,128]{1,0:T(8,128)S(1)}, u32[]{:S(2)}, u32[]{:S(2)}) collective-permute-start(f32[32,128]{1,0:T(8,128)S(1)} %get-tuple-element.37.refs_5_), channel_id=1, source_target_pairs={{0,4},{4,0},{8,12},{12,8},{16,20},{20,16},{24,28},{28,24},{32,36},... | collective-permute-start | bytes 49160 | tf_op jit(solution)/shard_map/ppermute | solution.py:357
  10.8 1.7 %collective-permute-start.4 = (f32[32,2048]{1,0:T(8,128)S(1)}, f32[32,2048]{1,0:T(8,128)S(1)}, u32[]{:S(2)}, u32[]{:S(2)}) collective-permute-start(f32[32,2048]{1,0:T(8,128)S(1)} %get-tuple-element.41.refs_2_), channel_id=1, source_target_pairs={{0,1},{1,0},{2,3},{3,2},{4,5},{5,4},{6,7},{7,6},{8,9},{9,8},{10,11... | collective-permute-start | bytes 786440 | tf_op jit(solution)/shard_map/ppermute | solution.py:354
  15.4 24.6 %collective-permute-start.6 = (bf16[2048,512]{1,0:T(8,128)(2,1)S(1)}, bf16[2048,512]{1,0:T(8,128)(2,1)S(1)}, u32[]{:S(2)}, u32[]{:S(2)}) collective-permute-start(bf16[2048,512]{1,0:T(8,128)(2,1)S(1)} %get-tuple-element.46), channel_id=1, source_target_pairs={{0,1},{1,0},{2,3},{3,2},{4,5},{5,4},{6,7},{7,6},{8,9},{9,8},{10,11... | collective-permute-start | bytes 6291464 | tf_op jit(solution)/shard_map/ppermute | solution.py:354
  15.7 9.4 %collective-permute-start.8 = (bf16[256,512]{1,0:T(8,128)(2,1)S(1)}, bf16[256,512]{1,0:T(8,128)(2,1)S(1)}, u32[]{:S(2)}, u32[]{:S(2)}) collective-permute-start(bf16[256,512]{1,0:T(8,128)(2,1)S(1)} %get-tuple-element.45), channel_id=1, source_target_pairs={{0,2},{1,3},{2,0},{3,1},{4,6},{5,7},{6,4},{7,5},{8,10},{9,11},{10,... | collective-permute-start | bytes 786440 | tf_op jit(solution)/shard_map/ppermute | solution.py:354
  20.1 5.0 %collective-permute-start.7 = (f32[32,128]{1,0:T(8,128)S(1)}, f32[32,128]{1,0:T(8,128)S(1)}, u32[]{:S(2)}, u32[]{:S(2)}) collective-permute-start(f32[32,128]{1,0:T(8,128)S(1)} %get-tuple-element.50), channel_id=1, source_target_pairs={{0,12},{4,8},{8,4},{12,0},{16,28},{20,24},{24,20},{28,16},{32,44},... | collective-permute-start | bytes 49160 | tf_op jit(solution)/shard_map/ppermute | solution.py:357
  22.3 9.4 %collective-permute-start.10 = (bf16[256,512]{1,0:T(8,128)(2,1)S(1)}, bf16[256,512]{1,0:T(8,128)(2,1)S(1)}, u32[]{:S(2)}, u32[]{:S(2)}) collective-permute-start(bf16[256,512]{1,0:T(8,128)(2,1)S(1)} %get-tuple-element.49), channel_id=1, source_target_pairs={{0,2},{1,3},{2,0},{3,1},{4,6},{5,7},{6,4},{7,5},{8,10},{9,11},{10,... | collective-permute-start | bytes 786440 | tf_op jit(solution)/shard_map/ppermute | solution.py:354
  27.9 3.8 %collective-permute-start.9 = (f32[32,128]{1,0:T(8,128)S(1)}, f32[32,128]{1,0:T(8,128)S(1)}, u32[]{:S(2)}, u32[]{:S(2)}) collective-permute-start(f32[32,128]{1,0:T(8,128)S(1)} %add.48.refs_6_), channel_id=1, source_target_pairs={{0,32},{4,36},{8,40},{12,44},{16,48},{20,52},{24,56},{28,60},{32,0... | collective-permute-start | bytes 49160 | tf_op jit(solution)/shard_map/ppermute | solution.py:357
  29.9 12.5 %collective-permute-start.11 = (bf16[256,512]{1,0:T(8,128)(2,1)S(1)}, bf16[256,512]{1,0:T(8,128)(2,1)S(1)}, u32[]{:S(2)}, u32[]{:S(2)}) collective-permute-start(bf16[256,512]{1,0:T(8,128)(2,1)S(1)} %get-tuple-element.52), channel_id=1, source_target_pairs={{0,2},{1,3},{2,0},{3,1},{4,6},{5,7},{6,4},{7,5},{8,10},{9,11},{10,... | collective-permute-start | bytes 786440 | tf_op jit(solution)/shard_map/ppermute | solution.py:354
  34.5 7.9 %collective-permute-start.12 = (f32[32,128]{1,0:T(8,128)S(1)}, f32[32,128]{1,0:T(8,128)S(1)}, u32[]{:S(2)}, u32[]{:S(2)}) collective-permute-start(f32[32,128]{1,0:T(8,128)S(1)} %add.49.refs_6_.refs_11_), channel_id=1, source_target_pairs={{0,96},{4,100},{8,104},{12,108},{16,112},{20,116},{24,120},{28,124... | collective-permute-start | bytes 49160 | tf_op jit(solution)/shard_map/ppermute | solution.py:357
  38.6 6.6 %collective-permute-start.13 = (bf16[256,512]{1,0:T(8,128)(2,1)S(1)}, bf16[256,512]{1,0:T(8,128)(2,1)S(1)}, u32[]{:S(2)}, u32[]{:S(2)}) collective-permute-start(bf16[256,512]{1,0:T(8,128)(2,1)S(1)} %get-tuple-element.57.refs_6_), channel_id=1, source_target_pairs={{0,2},{1,3},{2,0},{3,1},{4,6},{5,7},{6,4},{7,5},{8,10},{9,11},{10,... | collective-permute-start | bytes 786440 | tf_op jit(solution)/shard_map/ppermute | solution.py:354
  46.7 3.7 %collective-permute-start.15 = (f32[16,128]{1,0:T(8,128)S(1)}, f32[16,128]{1,0:T(8,128)S(1)}, u32[]{:S(2)}, u32[]{:S(2)}) collective-permute-start(f32[16,128]{1,0:T(8,128)S(1)} %pad_maximum_fusion), channel_id=1, source_target_pairs={{0,2},{1,3},{2,0},{3,1},{4,6},{5,7},{6,4},{7,5},{8,10},{9,11},{10,... | collective-permute-start | bytes 24584 | tf_op jit(solution)/shard_map/ppermute | solution.py:354
  51.3 1.3 %collective-permute-start.16 = (f32[56,128]{1,0:T(8,128)S(1)}, f32[56,128]{1,0:T(8,128)S(1)}, u32[]{:S(2)}, u32[]{:S(2)}) collective-permute-start(f32[56,128]{1,0:T(8,128)S(1)} %get-tuple-element.66), channel_id=1, source_target_pairs={{0,1},{1,0},{2,3},{3,2},{4,5},{5,4},{6,7},{7,6},{8,9},{9,8},{10,11... | collective-permute-start | bytes 86024 | tf_op jit(solution)/shard_map/ppermute | solution.py:354
  52.6 3.9 %collective-permute-start.17 = (f32[56,128]{1,0:T(8,128)S(1)}, f32[56,128]{1,0:T(8,128)S(1)}, u32[]{:S(2)}, u32[]{:S(2)}) collective-permute-start(f32[56,128]{1,0:T(8,128)S(1)} %add.56), channel_id=1, source_target_pairs={{0,2},{1,3},{2,0},{3,1},{4,6},{5,7},{6,4},{7,5},{8,10},{9,11},{10,... | collective-permute-start | bytes 86024 | tf_op jit(solution)/shard_map/ppermute | solution.py:354
  56.5 5.1 %collective-permute-start.18 = (f32[56,128]{1,0:T(8,128)S(1)}, f32[56,128]{1,0:T(8,128)S(1)}, u32[]{:S(2)}, u32[]{:S(2)}) collective-permute-start(f32[56,128]{1,0:T(8,128)S(1)} %add.57.refs_0_), channel_id=1, source_target_pairs={{0,18},{1,19},{2,16},{3,17},{4,22},{5,23},{6,20},{7,21},{8,26},{9,... | collective-permute-start | bytes 86024 | tf_op jit(solution)/shard_map/ppermute | solution.py:515
  61.6 4.9 %collective-permute-start.21 = (f32[24,128]{1,0:T(8,128)S(1)}, f32[24,128]{1,0:T(8,128)S(1)}, u32[]{:S(2)}, u32[]{:S(2)}) collective-permute-start(f32[24,128]{1,0:T(8,128)S(1)} %shard_map.125), channel_id=1, source_target_pairs={{0,12},{4,8},{8,4},{12,0},{16,28},{20,24},{24,20},{28,16},{32,44},... | collective-permute-start | bytes 36872 | tf_op jit(solution)/shard_map/ppermute | solution.py:357
  63.8 5.2 %collective-permute-start.20 = (f32[24,128]{1,0:T(8,128)S(1)}, f32[24,128]{1,0:T(8,128)S(1)}, u32[]{:S(2)}, u32[]{:S(2)}) collective-permute-start(f32[24,128]{1,0:T(8,128)S(1)} %shard_map.125), channel_id=1, source_target_pairs={{0,8},{4,12},{8,0},{12,4},{16,24},{20,28},{24,16},{28,20},{32,40},... | collective-permute-start | bytes 36872 | tf_op jit(solution)/shard_map/ppermute | solution.py:357
  64.5 4.4 %collective-permute-start.19 = (f32[24,128]{1,0:T(8,128)S(1)}, f32[24,128]{1,0:T(8,128)S(1)}, u32[]{:S(2)}, u32[]{:S(2)}) collective-permute-start(f32[24,128]{1,0:T(8,128)S(1)} %shard_map.125), channel_id=1, source_target_pairs={{0,4},{4,0},{8,12},{12,8},{16,20},{20,16},{24,28},{28,24},{32,36},... | collective-permute-start | bytes 36872 | tf_op jit(solution)/shard_map/ppermute | solution.py:357
  69.0 5.0 %collective-permute-start.24 = (f32[24,128]{1,0:T(8,128)S(1)}, f32[24,128]{1,0:T(8,128)S(1)}, u32[]{:S(2)}, u32[]{:S(2)}) collective-permute-start(f32[24,128]{1,0:T(8,128)S(1)} %add_add_fusion.1), channel_id=1, source_target_pairs={{0,96},{4,100},{8,104},{12,108},{16,112},{20,116},{24,120},{28,124... | collective-permute-start | bytes 36872 | tf_op jit(solution)/shard_map/ppermute | solution.py:357
  70.2 5.2 %collective-permute-start.23 = (f32[24,128]{1,0:T(8,128)S(1)}, f32[24,128]{1,0:T(8,128)S(1)}, u32[]{:S(2)}, u32[]{:S(2)}) collective-permute-start(f32[24,128]{1,0:T(8,128)S(1)} %add_add_fusion.1), channel_id=1, source_target_pairs={{0,64},{4,68},{8,72},{12,76},{16,80},{20,84},{24,88},{28,92},{32,9... | collective-permute-start | bytes 36872 | tf_op jit(solution)/shard_map/ppermute | solution.py:357
  70.9 4.4 %collective-permute-start.22 = (f32[24,128]{1,0:T(8,128)S(1)}, f32[24,128]{1,0:T(8,128)S(1)}, u32[]{:S(2)}, u32[]{:S(2)}) collective-permute-start(f32[24,128]{1,0:T(8,128)S(1)} %add_add_fusion.1), channel_id=1, source_target_pairs={{0,32},{4,36},{8,40},{12,44},{16,48},{20,52},{24,56},{28,60},{32,0... | collective-permute-start | bytes 36872 | tf_op jit(solution)/shard_map/ppermute | solution.py:357
  (6 other events, 27.2 us)
where the time goes:
time: 76.9 us; the launch traced here: 76.8 us
  starting transfers between devices  30.5 us (40%)
  Pallas kernels  26.4 us (34%)
  waiting for transfers between devices  18.9 us (25%)
  between operations  0.88 us (1%)
    pallas_call x14, Pallas kernels, call(): pl.pallas_call(run, out_shape=out_shape, in_specs=in_specs, out_specs=jax...  26.4 us
    ppermute x10, starting transfers between devices, over_member(): return lax.ppermute(x, 'member', [(i, i ^ k) for i in range(members)])  18.2 us
    ppermute x14, starting transfers between devices, over_tensor(): return lax.ppermute(x, 'tensor', [(i, i ^ k) for i in range(4)])  10 us
    ppermute x10, waiting for transfers between devices, over_member(): return lax.ppermute(x, 'member', [(i, i ^ k) for i in range(members)])  8.36 us
    ppermute x14, waiting for transfers between devices, over_tensor(): return lax.ppermute(x, 'tensor', [(i, i ^ k) for i in range(4)])  7.68 us
    ppermute x1, waiting for transfers between devices, per_device(): met = lax.ppermute(total, ('member', 'tensor'), pairs)  2.84 us
    ppermute x1, starting transfers between devices, per_device(): met = lax.ppermute(total, ('member', 'tensor'), pairs)  2.24 us
  transfers between devices with their start and end apart: 25, of which 11 were waited for; matrix products, arithmetic and copies ran while one was open for 0% of the time, Pallas kernels for 25%

commit v1 on v0

--- a/solution.py
+++ b/solution.py
@@ -14,7 +14,7 @@
 KCAT = 256
 MIB = 1 << 20
 US = 10**9
-GROUPS = ((0, 2), (2, 4), (4, 6), (6, 8))
+GROUPS = ((0, 1), (1, 3), (3, 5), (5, 7), (7, 8))
 
 
 def split3(x):
@@ -233,8 +233,8 @@
     return x + dot(q[group[0] : group[1]].reshape((group[1] - group[0]) * WIN, KCAT), ecat[0])
 
 
-def home_kernel(q, ecat, d_own, d_peer, a0, a1, part):
-    for group, act in zip(GROUPS[:2], (a0, a1)):
+def home_kernel(q, ecat, d_own, d_peer, a0, a1, a2, part):
+    for group, act in zip(GROUPS[:3], (a0, a1, a2)):
         part[WIN * group[0] : WIN * group[1], :] = home_rows(group, q, ecat, d_own, d_peer, act)
 
 
@@ -251,16 +251,13 @@
     return jnp.where(row == 0, rows[0], jnp.where(row == 1, rows[1], 0.0))
 
 
-def state_kernel(
-    members, own, q, ecat, d_own, d_peer, a2, a3, part, c0, c1, c2, info, mine, late, state, last, stats, shares
-):
-    shares[...] = weights(info, mine[...] + late[...], members, own)
-    last[...] = home_rows(GROUPS[3], q, ecat, d_own, d_peer, a3)
+def state_kernel(q, ecat, d_own, d_peer, a3, a4, part, c0, c1, c2, c3, state, last, stats):
+    last[...] = home_rows(GROUPS[4], q, ecat, d_own, d_peer, a4)
     table = jnp.zeros((WIN, WIN), F32)
-    for g, cross in enumerate((c0, c1, c2)):
+    for g, cross in enumerate((c0, c1, c2, c3)):
         group = GROUPS[g]
         rows = slice(WIN * group[0], WIN * group[1])
-        x = part[rows, :] if g < 2 else home_rows(group, q, ecat, d_own, d_peer, a2)
+        x = part[rows, :] if g < 3 else home_rows(group, q, ecat, d_own, d_peer, a3)
         x = x + cross[...].astype(F32)
         state[rows, :] = x
         for i, p in enumerate(range(*group)):
@@ -268,18 +265,19 @@
     stats[...] = table.T[: 2 * PATCHES]
 
 
-def last_state_kernel(last, cross, prev, state, stats):
+def last_state_kernel(members, own, last, cross, prev, info, mine, late, state, stats, shares):
     x = last[...] + cross[...].astype(F32)
     state[...] = x
     table = jnp.zeros((WIN, WIN), F32)
-    for i, p in enumerate(range(*GROUPS[3])):
+    for i, p in enumerate(range(*GROUPS[4])):
         table = add_stats(table, p, x[i * WIN : (i + 1) * WIN])
     stats[...] = prev[...] + table.T[: 2 * PATCHES]
+    shares[...] = weights(info, mine[...] + late[...], members, own)
 
 
 def head_kernel(stats, state, last, heads, shard, shares, send, keep, scr):
     core = lax.axis_index("tensor") & 1
-    first = GROUPS[3][0]
+    first = GROUPS[4][0]
     scale = lax.rsqrt(stats[PATCHES:, :] * (1.0 / D) + 1e-05)
     table = jnp.concatenate([stats[:PATCHES, :], scale, jnp.zeros((WIN - 2 * PATCHES, WIN), F32)], axis=0).T
     total = jnp.zeros((WIN, HORIZONS), F32)
@@ -445,7 +443,7 @@
     acts, crossed = [act], [over_tensor(send, 2)]
     fed = (q, rstd, m_own, m_peer, down[0], peer_x)
     peer_y = over_tensor(lax.optimization_barrier((give_y, send))[0], 1)
-    for g in range(1, 4):
+    for g in range(1, 5):
         act, send = call(
             functools.partial(away_kernel, GROUPS[g]),
             sums(GROUPS[g]),
@@ -457,38 +455,37 @@
         )
         acts.append(act)
         crossed.append(over_tensor(send, 2))
-        if g < 3:
+        if g in (2, 3):
             every = hop(every, send)
     every, late = hop_parts(every, send)
     homes = (q, ecat, down[0], peer_y)
     (part,) = call(
         home_kernel,
-        (pltpu.VMEM((GROUPS[1][1] * WIN, SHARD), F32),),
-        [V] * 6,
-        (*homes, *acts[:2]),
+        (pltpu.VMEM((GROUPS[2][1] * WIN, SHARD), F32),),
+        [V] * 7,
+        (*homes, *acts[:3]),
         US // 10,
         1000,
         after=(send,),
     )
-    tail = (GROUPS[3][1] - GROUPS[3][0]) * WIN
-    state, last, stats, shares = call(
-        functools.partial(state_kernel, members, own),
+    tail = (GROUPS[4][1] - GROUPS[4][0]) * WIN
+    state, last, stats = call(
+        state_kernel,
         (
-            pltpu.VMEM((GROUPS[2][1] * WIN, SHARD), F32),
+            pltpu.VMEM((GROUPS[3][1] * WIN, SHARD), F32),
             pltpu.VMEM((tail, SHARD), F32),
             pltpu.VMEM((2 * PATCHES, WIN), F32),
-            pltpu.VMEM((8, WIN), F32),
         ),
-        [V] * 13,
-        (*homes, *acts[2:], part, *crossed[:3], info, every, late),
+        [V] * 11,
+        (*homes, *acts[3:], part, *crossed[:4]),
         5 * US,
         1000,
     )
-    last, stats = call(
-        last_state_kernel,
-        (pltpu.VMEM((tail, SHARD), F32), pltpu.VMEM((2 * PATCHES, WIN), F32)),
-        [V] * 3,
-        (last, crossed[3], stats),
+    last, stats, shares = call(
+        functools.partial(last_state_kernel, members, own),
+        (pltpu.VMEM((tail, SHARD), F32), pltpu.VMEM((2 * PATCHES, WIN), F32), pltpu.VMEM((8, WIN), F32)),
+        [V] * 6,
+        (last, crossed[4], stats, info, every, late),
         US,
         1000,
     )

time: 76.9 us -> 78.2 us (1.017)
  starting transfers between devices: 30.5 us -> 31.5 us
    ppermute x14 -> x15, waiting for transfers between devices: 7.68 us -> 9.55 us  [over_tensor(): return lax.ppermute(x, 'tensor', [(i, i ^ k) for i in range(4)])]
    ppermute x10, waiting for transfers between devices: 8.36 us -> 6.52 us  [over_member(): return lax.ppermute(x, 'member', [(i, i ^ k) for i in range(members)])]
    ppermute x14 -> x15, starting transfers between devices: 10 us -> 11.3 us  [over_tensor(): return lax.ppermute(x, 'tensor', [(i, i ^ k) for i in range(4)])]
    pallas_call x14 -> x15, Pallas kernels: 26.4 us -> 26.6 us  [call(): pl.pallas_call(run, out_shape=out_shape, in_specs=in_specs, out_specs=jax...]
  transfers between devices with their start and end apart: 25 -> 26, of which waited for: 11 -> 13; matrix products, arithmetic and copies ran while one was open for 0% -> 0% of each run, Pallas kernels for 25% -> 27%
where the time goes in v1:
time: 78.2 us; the launch traced here: 78.1 us
  starting transfers between devices  31.5 us (40%)
  Pallas kernels  26.6 us (34%)
  waiting for transfers between devices  19 us (24%)
  between operations  0.89 us (1%)
    pallas_call x15, Pallas kernels, call(): pl.pallas_call(run, out_shape=out_shape, in_specs=in_specs, out_specs=jax...  26.6 us
    ppermute x10, starting transfers between devices, over_member(): return lax.ppermute(x, 'member', [(i, i ^ k) for i in range(members)])  18.1 us
    ppermute x15, starting transfers between devices, over_tensor(): return lax.ppermute(x, 'tensor', [(i, i ^ k) for i in range(4)])  11.3 us
    ppermute x15, waiting for transfers between devices, over_tensor(): return lax.ppermute(x, 'tensor', [(i, i ^ k) for i in range(4)])  9.55 us
    ppermute x10, waiting for transfers between devices, over_member(): return lax.ppermute(x, 'member', [(i, i ^ k) for i in range(members)])  6.52 us
    ppermute x1, waiting for transfers between devices, per_device(): met = lax.ppermute(total, ('member', 'tensor'), pairs)  2.9 us
    ppermute x1, starting transfers between devices, per_device(): met = lax.ppermute(total, ('member', 'tensor'), pairs)  2.18 us
  transfers between devices with their start and end apart: 26, of which 13 were waited for; matrix products, arithmetic and copies ran while one was open for 0% of the time, Pallas kernels for 27%

profile of v1, /device:TPU:0, one launch (start us, length us, event | category | flops | bytes accessed | tf_op | source)
XLA Modules:
  0.0 78.1 jit_solution(8377172915780230286)
XLA Ops:
  0.6 1.9 %shard_map.113 = (f32[32,512]{1,0:T(8,128)S(1)}, f32[32,128]{1,0:T(8,128)S(1)}, bf16[2048,512]{1,0:T(8,128)(2,1)S(1)}) custom-call(f32[1,16,512]{2,1,0:T(8,128)} %refs_0_.1, f32[1,8,512]{2,1,0:T(8,128)} %refs_1_.1, f32[1,512]{1,0:T(1,128)} %refs_2_.2, f32[1,512]{1,0:T(1,128)} %refs_3_.1, s32[4,32]{1,0:T(4,128)} %bitcast.21, bf16[1,2048,2048]{2,1,0:T(8,128)(2,1)} %refs_2_.3), custom_call_target="tpu_custom_call" | custom-call | flops 2000000000 | bytes 1000 | tf_op jit(solution)/shard_map/pallas_call | solution.py:53
  2.6 1.8 %collective-permute-start.2 = (f32[32,512]{1,0:T(8,128)S(1)}, f32[32,512]{1,0:T(8,128)S(1)}, u32[]{:S(2)}, u32[]{:S(2)}) collective-permute-start(f32[32,512]{1,0:T(8,128)S(1)} %get-tuple-element.37.refs_3_.refs_1_.refs_4_), channel_id=1, source_target_pairs={{0,3},{1,2},{2,1},{3,0},{4,7},{5,6},{6,5},{7,4},{8,11},{9,10},{10,... | collective-permute-start | bytes 196616 | tf_op jit(solution)/shard_map/ppermute | solution.py:352
  4.8 1.6 %collective-permute-start.3 = (f32[32,128]{1,0:T(8,128)S(1)}, f32[32,128]{1,0:T(8,128)S(1)}, u32[]{:S(2)}, u32[]{:S(2)}) collective-permute-start(f32[32,128]{1,0:T(8,128)S(1)} %get-tuple-element.39.refs_5_), channel_id=1, source_target_pairs={{0,4},{4,0},{8,12},{12,8},{16,20},{20,16},{24,28},{28,24},{32,36},... | collective-permute-start | bytes 49160 | tf_op jit(solution)/shard_map/ppermute | solution.py:355
  6.4 2.7 %shard_map.114 = (bf16[2048,512]{1,0:T(8,128)(2,1)S(1)}, bf16[8,128,256]{2,1,0:T(8,128)(2,1)S(1)}, f32[8,128]{1,0:T(8,128)S(1)}, f32[128,128]{1,0:T(8,128)S(1)}) custom-call(f32[128,128]{1,0:T(8,128)} %bitcast.22, s32[1,128]{1,0:T(1,128)} %bitcast.23, bf16[1,2048,2048]{2,1,0:T(8,128)(2,1)} %refs_2_.3, f32[32,512]{1,0:T(8,128)S(1)} %get-tuple-element.37.refs_3_.refs_1_.refs_4_), custom_call_target="tpu_custom_call" | custom-call | flops 5000000000 | bytes 1000 | tf_op jit(solution)/shard_map/pallas_call | solution.py:53
  14.3 1.6 %collective-permute-start.7 = (bf16[128,512]{1,0:T(8,128)(2,1)S(1)}, bf16[128,512]{1,0:T(8,128)(2,1)S(1)}, u32[]{:S(2)}, u32[]{:S(2)}) collective-permute-start(bf16[128,512]{1,0:T(8,128)(2,1)S(1)} %get-tuple-element.47), channel_id=1, source_target_pairs={{0,2},{1,3},{2,0},{3,1},{4,6},{5,7},{6,4},{7,5},{8,10},{9,11},{10,... | collective-permute-start | bytes 393224 | tf_op jit(solution)/shard_map/ppermute | solution.py:352
  15.9 2.8 %shard_map.119 = (bf16[256,4096]{1,0:T(8,128)(2,1)S(1)}, bf16[256,512]{1,0:T(8,128)(2,1)S(1)}) custom-call(bf16[8,128,256]{2,1,0:T(8,128)(2,1)S(1)} %get-tuple-element.38.refs_0_, f32[8,128,128]{2,1,0:T(8,128)S(1)} %get-tuple-element.44.refs_1_, bf16[256,2048]{1,0:T(8,128)(2,1)S(1)} %get-tuple-element.45.refs_2_, ...), custom_call_target="tpu_custom_call" | custom-call | flops 4000000000 | bytes 1000 | tf_op jit(solution)/shard_map/pallas_call | solution.py:53
  20.0 2.8 %shard_map.118 = (bf16[256,4096]{1,0:T(8,128)(2,1)S(1)}, bf16[256,512]{1,0:T(8,128)(2,1)S(1)}) custom-call(bf16[8,128,256]{2,1,0:T(8,128)(2,1)S(1)} %get-tuple-element.38.refs_0_, f32[8,128,128]{2,1,0:T(8,128)S(1)} %get-tuple-element.44.refs_1_, bf16[256,2048]{1,0:T(8,128)(2,1)S(1)} %get-tuple-element.45.refs_2_, ...), custom_call_target="tpu_custom_call" | custom-call | flops 4000000000 | bytes 1000 | tf_op jit(solution)/shard_map/pallas_call | solution.py:53
  22.8 2.2 %collective-permute-start.8 = (f32[32,128]{1,0:T(8,128)S(1)}, f32[32,128]{1,0:T(8,128)S(1)}, u32[]{:S(2)}, u32[]{:S(2)}) collective-permute-start(f32[32,128]{1,0:T(8,128)S(1)} %get-tuple-element.52.refs_6_), channel_id=1, source_target_pairs={{0,12},{4,8},{8,4},{12,0},{16,28},{20,24},{24,20},{28,16},{32,44},... | collective-permute-start | bytes 49160 | tf_op jit(solution)/shard_map/ppermute | solution.py:355
  27.8 2.8 %shard_map.120 = (bf16[256,4096]{1,0:T(8,128)(2,1)S(1)}, bf16[256,512]{1,0:T(8,128)(2,1)S(1)}) custom-call(bf16[8,128,256]{2,1,0:T(8,128)(2,1)S(1)} %get-tuple-element.38.refs_0_, f32[8,128,128]{2,1,0:T(8,128)S(1)} %get-tuple-element.44.refs_1_, bf16[256,2048]{1,0:T(8,128)(2,1)S(1)} %get-tuple-element.45.refs_2_, ...), custom_call_target="tpu_custom_call" | custom-call | flops 4000000000 | bytes 1000 | tf_op jit(solution)/shard_map/pallas_call | solution.py:53
  30.6 2.0 %collective-permute-start.10 = (f32[32,128]{1,0:T(8,128)S(1)}, f32[32,128]{1,0:T(8,128)S(1)}, u32[]{:S(2)}, u32[]{:S(2)}) collective-permute-start(f32[32,128]{1,0:T(8,128)S(1)} %add.48.refs_6_), channel_id=1, source_target_pairs={{0,32},{4,36},{8,40},{12,44},{16,48},{20,52},{24,56},{28,60},{32,0... | collective-permute-start | bytes 49160 | tf_op jit(solution)/shard_map/ppermute | solution.py:355
  32.6 1.6 %collective-permute-start.12 = (bf16[256,512]{1,0:T(8,128)(2,1)S(1)}, bf16[256,512]{1,0:T(8,128)(2,1)S(1)}, u32[]{:S(2)}, u32[]{:S(2)}) collective-permute-start(bf16[256,512]{1,0:T(8,128)(2,1)S(1)} %get-tuple-element.55), channel_id=1, source_target_pairs={{0,2},{1,3},{2,0},{3,1},{4,6},{5,7},{6,4},{7,5},{8,10},{9,11},{10,... | collective-permute-start | bytes 786440 | tf_op jit(solution)/shard_map/ppermute | solution.py:352
  35.9 1.7 %collective-permute-start.13 = (bf16[128,512]{1,0:T(8,128)(2,1)S(1)}, bf16[128,512]{1,0:T(8,128)(2,1)S(1)}, u32[]{:S(2)}, u32[]{:S(2)}) collective-permute-start(bf16[128,512]{1,0:T(8,128)(2,1)S(1)} %get-tuple-element.61.refs_7_), channel_id=1, source_target_pairs={{0,2},{1,3},{2,0},{3,1},{4,6},{5,7},{6,4},{7,5},{8,10},{9,11},{10,... | collective-permute-start | bytes 393224 | tf_op jit(solution)/shard_map/ppermute | solution.py:352
  37.5 4.0 %collective-permute-start.14 = (f32[32,128]{1,0:T(8,128)S(1)}, f32[32,128]{1,0:T(8,128)S(1)}, u32[]{:S(2)}, u32[]{:S(2)}) collective-permute-start(f32[32,128]{1,0:T(8,128)S(1)} %add.49.refs_6_.refs_4_), channel_id=1, source_target_pairs={{0,96},{4,100},{8,104},{12,108},{16,112},{20,116},{24,120},{28,124... | collective-permute-start | bytes 49160 | tf_op jit(solution)/shard_map/ppermute | solution.py:355
  41.6 3.1 %shard_map.122.refs_6_ = f32[640,512]{1,0:T(8,128)S(1)} custom-call(bf16[8,128,256]{2,1,0:T(8,128)(2,1)S(1)} %get-tuple-element.38.refs_0_, bf16[4,256,512]{2,1,0:T(8,128)(2,1)S(1)} %get-tuple-element.41.refs_1_, bf16[2048,2048]{1,0:T(8,128)(2,1)S(1)} %bitcast.15, bf16[2048,512]{1,0:T(8,128)(2,1)S(1)} %collective-permute-done.6.refs_3_, ...), custom_call_target="tpu_custom_call" | custom-call | flops 100000000 | bytes 1000 | tf_op jit(solution)/shard_map/pallas_call | solution.py:53
  44.6 2.2 %shard_map.123 = (f32[896,512]{1,0:T(8,128)S(1)}, f32[128,512]{1,0:T(8,128)S(1)}, f32[16,128]{1,0:T(8,128)S(1)}) custom-call(bf16[8,128,256]{2,1,0:T(8,128)(2,1)S(1)} %get-tuple-element.38.refs_0_, bf16[4,256,512]{2,1,0:T(8,128)(2,1)S(1)} %get-tuple-element.41.refs_1_, bf16[2048,2048]{1,0:T(8,128)(2,1)S(1)} %bitcast.16, ...), custom_call_target="tpu_custom_call" | custom-call | flops 5000000000 | bytes 1000 | tf_op jit(solution)/shard_map/pallas_call | solution.py:53
  49.1 3.2 %collective-permute-done.16 = f32[16,128]{1,0:T(8,128)S(1)} collective-permute-done((f32[16,128]{1,0:T(8,128)S(1)}, f32[16,128]{1,0:T(8,128)S(1)}, u32[]{:S(2)}, u32[]{:S(2)}) %collective-permute-start.16) | collective-permute-done | bytes 8224 | tf_op jit(solution)/shard_map/ppermute | solution.py:352
  54.9 3.4 %collective-permute-done.18 = f32[56,128]{1,0:T(8,128)S(1)} collective-permute-done((f32[56,128]{1,0:T(8,128)S(1)}, f32[56,128]{1,0:T(8,128)S(1)}, u32[]{:S(2)}, u32[]{:S(2)}) %collective-permute-start.18) | collective-permute-done | bytes 28704 | tf_op jit(solution)/shard_map/ppermute | solution.py:352
  58.4 2.2 %collective-permute-start.19 = (f32[56,128]{1,0:T(8,128)S(1)}, f32[56,128]{1,0:T(8,128)S(1)}, u32[]{:S(2)}, u32[]{:S(2)}) collective-permute-start(f32[56,128]{1,0:T(8,128)S(1)} %add.57.refs_0_), channel_id=1, source_target_pairs={{0,18},{1,19},{2,16},{3,17},{4,22},{5,23},{6,20},{7,21},{8,26},{9,... | collective-permute-start | bytes 86024 | tf_op jit(solution)/shard_map/ppermute | solution.py:512
  60.5 2.9 %collective-permute-done.19.refs_1_ = f32[56,128]{1,0:T(8,128)S(1)} collective-permute-done((f32[56,128]{1,0:T(8,128)S(1)}, f32[56,128]{1,0:T(8,128)S(1)}, u32[]{:S(2)}, u32[]{:S(2)}) %collective-permute-start.19) | collective-permute-done | bytes 28704 | tf_op jit(solution)/shard_map/ppermute | solution.py:512
  63.4 2.1 %collective-permute-start.22 = (f32[24,128]{1,0:T(8,128)S(1)}, f32[24,128]{1,0:T(8,128)S(1)}, u32[]{:S(2)}, u32[]{:S(2)}) collective-permute-start(f32[24,128]{1,0:T(8,128)S(1)} %shard_map.126), channel_id=1, source_target_pairs={{0,12},{4,8},{8,4},{12,0},{16,28},{20,24},{24,20},{28,16},{32,44},... | collective-permute-start | bytes 36872 | tf_op jit(solution)/shard_map/ppermute | solution.py:355
  65.5 2.0 %collective-permute-start.20 = (f32[24,128]{1,0:T(8,128)S(1)}, f32[24,128]{1,0:T(8,128)S(1)}, u32[]{:S(2)}, u32[]{:S(2)}) collective-permute-start(f32[24,128]{1,0:T(8,128)S(1)} %shard_map.126), channel_id=1, source_target_pairs={{0,4},{4,0},{8,12},{12,8},{16,20},{20,16},{24,28},{28,24},{32,36},... | collective-permute-start | bytes 36872 | tf_op jit(solution)/shard_map/ppermute | solution.py:355
  68.3 2.4 %collective-permute-done.21 = f32[24,128]{1,0:T(8,128)S(1)} collective-permute-done((f32[24,128]{1,0:T(8,128)S(1)}, f32[24,128]{1,0:T(8,128)S(1)}, u32[]{:S(2)}, u32[]{:S(2)}) %collective-permute-start.21) | collective-permute-done | bytes 12320 | tf_op jit(solution)/shard_map/ppermute | solution.py:355
  70.8 1.9 %collective-permute-start.24 = (f32[24,128]{1,0:T(8,128)S(1)}, f32[24,128]{1,0:T(8,128)S(1)}, u32[]{:S(2)}, u32[]{:S(2)}) collective-permute-start(f32[24,128]{1,0:T(8,128)S(1)} %add_add_fusion.1), channel_id=1, source_target_pairs={{0,64},{4,68},{8,72},{12,76},{16,80},{20,84},{24,88},{28,92},{32,9... | collective-permute-start | bytes 36872 | tf_op jit(solution)/shard_map/ppermute | solution.py:355
  72.7 2.2 %collective-permute-start.23 = (f32[24,128]{1,0:T(8,128)S(1)}, f32[24,128]{1,0:T(8,128)S(1)}, u32[]{:S(2)}, u32[]{:S(2)}) collective-permute-start(f32[24,128]{1,0:T(8,128)S(1)} %add_add_fusion.1), channel_id=1, source_target_pairs={{0,32},{4,36},{8,40},{12,44},{16,48},{20,52},{24,56},{28,60},{32,0... | collective-permute-start | bytes 36872 | tf_op jit(solution)/shard_map/ppermute | solution.py:355
  (65 shorter events, 20.3 us)
Async XLA Ops:
  2.5 9.9 %collective-permute-start.5 = (bf16[2048,512]{1,0:T(8,128)(2,1)S(1)}, bf16[2048,512]{1,0:T(8,128)(2,1)S(1)}, u32[]{:S(2)}, u32[]{:S(2)}) collective-permute-start(bf16[2048,512]{1,0:T(8,128)(2,1)S(1)} %get-tuple-element.46), channel_id=1, source_target_pairs={{0,1},{1,0},{2,3},{3,2},{4,5},{5,4},{6,7},{7,6},{8,9},{9,8},{10,11... | collective-permute-start | bytes 6291464 | tf_op jit(solution)/shard_map/ppermute | solution.py:352
  2.6 6.5 %collective-permute-start.2 = (f32[32,512]{1,0:T(8,128)S(1)}, f32[32,512]{1,0:T(8,128)S(1)}, u32[]{:S(2)}, u32[]{:S(2)}) collective-permute-start(f32[32,512]{1,0:T(8,128)S(1)} %get-tuple-element.37.refs_3_.refs_1_.refs_4_), channel_id=1, source_target_pairs={{0,3},{1,2},{2,1},{3,0},{4,7},{5,6},{6,5},{7,4},{8,11},{9,10},{10,... | collective-permute-start | bytes 196616 | tf_op jit(solution)/shard_map/ppermute | solution.py:352
  4.4 4.7 %collective-permute-start.1 = (f32[32,512]{1,0:T(8,128)S(1)}, f32[32,512]{1,0:T(8,128)S(1)}, u32[]{:S(2)}, u32[]{:S(2)}) collective-permute-start(f32[32,512]{1,0:T(8,128)S(1)} %get-tuple-element.37.refs_3_.refs_1_.refs_4_), channel_id=1, source_target_pairs={{0,2},{1,3},{2,0},{3,1},{4,6},{5,7},{6,4},{7,5},{8,10},{9,11},{10,... | collective-permute-start | bytes 196616 | tf_op jit(solution)/shard_map/ppermute | solution.py:352
  4.8 4.4 %collective-permute-start = (f32[32,512]{1,0:T(8,128)S(1)}, f32[32,512]{1,0:T(8,128)S(1)}, u32[]{:S(2)}, u32[]{:S(2)}) collective-permute-start(f32[32,512]{1,0:T(8,128)S(1)} %get-tuple-element.37.refs_3_.refs_1_.refs_4_), channel_id=1, source_target_pairs={{0,1},{1,0},{2,3},{3,2},{4,5},{5,4},{6,7},{7,6},{8,9},{9,8},{10,11... | collective-permute-start | bytes 196616 | tf_op jit(solution)/shard_map/ppermute | solution.py:352
  4.8 4.3 %collective-permute-start.3 = (f32[32,128]{1,0:T(8,128)S(1)}, f32[32,128]{1,0:T(8,128)S(1)}, u32[]{:S(2)}, u32[]{:S(2)}) collective-permute-start(f32[32,128]{1,0:T(8,128)S(1)} %get-tuple-element.39.refs_5_), channel_id=1, source_target_pairs={{0,4},{4,0},{8,12},{12,8},{16,20},{20,16},{24,28},{28,24},{32,36},... | collective-permute-start | bytes 49160 | tf_op jit(solution)/shard_map/ppermute | solution.py:355
  10.8 1.7 %collective-permute-start.4 = (f32[32,2048]{1,0:T(8,128)S(1)}, f32[32,2048]{1,0:T(8,128)S(1)}, u32[]{:S(2)}, u32[]{:S(2)}) collective-permute-start(f32[32,2048]{1,0:T(8,128)S(1)} %get-tuple-element.43.refs_2_), channel_id=1, source_target_pairs={{0,1},{1,0},{2,3},{3,2},{4,5},{5,4},{6,7},{7,6},{8,9},{9,8},{10,11... | collective-permute-start | bytes 786440 | tf_op jit(solution)/shard_map/ppermute | solution.py:352
  14.0 27.6 %collective-permute-start.6 = (bf16[2048,512]{1,0:T(8,128)(2,1)S(1)}, bf16[2048,512]{1,0:T(8,128)(2,1)S(1)}, u32[]{:S(2)}, u32[]{:S(2)}) collective-permute-start(bf16[2048,512]{1,0:T(8,128)(2,1)S(1)} %get-tuple-element.48), channel_id=1, source_target_pairs={{0,1},{1,0},{2,3},{3,2},{4,5},{5,4},{6,7},{7,6},{8,9},{9,8},{10,11... | collective-permute-start | bytes 6291464 | tf_op jit(solution)/shard_map/ppermute | solution.py:352
  14.3 5.6 %collective-permute-start.7 = (bf16[128,512]{1,0:T(8,128)(2,1)S(1)}, bf16[128,512]{1,0:T(8,128)(2,1)S(1)}, u32[]{:S(2)}, u32[]{:S(2)}) collective-permute-start(bf16[128,512]{1,0:T(8,128)(2,1)S(1)} %get-tuple-element.47), channel_id=1, source_target_pairs={{0,2},{1,3},{2,0},{3,1},{4,6},{5,7},{6,4},{7,5},{8,10},{9,11},{10,... | collective-permute-start | bytes 393224 | tf_op jit(solution)/shard_map/ppermute | solution.py:352
  18.7 9.1 %collective-permute-start.9 = (bf16[256,512]{1,0:T(8,128)(2,1)S(1)}, bf16[256,512]{1,0:T(8,128)(2,1)S(1)}, u32[]{:S(2)}, u32[]{:S(2)}) collective-permute-start(bf16[256,512]{1,0:T(8,128)(2,1)S(1)} %get-tuple-element.53), channel_id=1, source_target_pairs={{0,2},{1,3},{2,0},{3,1},{4,6},{5,7},{6,4},{7,5},{8,10},{9,11},{10,... | collective-permute-start | bytes 786440 | tf_op jit(solution)/shard_map/ppermute | solution.py:352
  22.8 5.0 %collective-permute-start.8 = (f32[32,128]{1,0:T(8,128)S(1)}, f32[32,128]{1,0:T(8,128)S(1)}, u32[]{:S(2)}, u32[]{:S(2)}) collective-permute-start(f32[32,128]{1,0:T(8,128)S(1)} %get-tuple-element.52.refs_6_), channel_id=1, source_target_pairs={{0,12},{4,8},{8,4},{12,0},{16,28},{20,24},{24,20},{28,16},{32,44},... | collective-permute-start | bytes 49160 | tf_op jit(solution)/shard_map/ppermute | solution.py:355
  25.0 9.4 %collective-permute-start.11 = (bf16[256,512]{1,0:T(8,128)(2,1)S(1)}, bf16[256,512]{1,0:T(8,128)(2,1)S(1)}, u32[]{:S(2)}, u32[]{:S(2)}) collective-permute-start(bf16[256,512]{1,0:T(8,128)(2,1)S(1)} %get-tuple-element.51), channel_id=1, source_target_pairs={{0,2},{1,3},{2,0},{3,1},{4,6},{5,7},{6,4},{7,5},{8,10},{9,11},{10,... | collective-permute-start | bytes 786440 | tf_op jit(solution)/shard_map/ppermute | solution.py:352
  30.6 3.8 %collective-permute-start.10 = (f32[32,128]{1,0:T(8,128)S(1)}, f32[32,128]{1,0:T(8,128)S(1)}, u32[]{:S(2)}, u32[]{:S(2)}) collective-permute-start(f32[32,128]{1,0:T(8,128)S(1)} %add.48.refs_6_), channel_id=1, source_target_pairs={{0,32},{4,36},{8,40},{12,44},{16,48},{20,52},{24,56},{28,60},{32,0... | collective-permute-start | bytes 49160 | tf_op jit(solution)/shard_map/ppermute | solution.py:355
  32.6 12.1 %collective-permute-start.12 = (bf16[256,512]{1,0:T(8,128)(2,1)S(1)}, bf16[256,512]{1,0:T(8,128)(2,1)S(1)}, u32[]{:S(2)}, u32[]{:S(2)}) collective-permute-start(bf16[256,512]{1,0:T(8,128)(2,1)S(1)} %get-tuple-element.55), channel_id=1, source_target_pairs={{0,2},{1,3},{2,0},{3,1},{4,6},{5,7},{6,4},{7,5},{8,10},{9,11},{10,... | collective-permute-start | bytes 786440 | tf_op jit(solution)/shard_map/ppermute | solution.py:352
  35.9 11.0 %collective-permute-start.13 = (bf16[128,512]{1,0:T(8,128)(2,1)S(1)}, bf16[128,512]{1,0:T(8,128)(2,1)S(1)}, u32[]{:S(2)}, u32[]{:S(2)}) collective-permute-start(bf16[128,512]{1,0:T(8,128)(2,1)S(1)} %get-tuple-element.61.refs_7_), channel_id=1, source_target_pairs={{0,2},{1,3},{2,0},{3,1},{4,6},{5,7},{6,4},{7,5},{8,10},{9,11},{10,... | collective-permute-start | bytes 393224 | tf_op jit(solution)/shard_map/ppermute | solution.py:352
  37.5 9.4 %collective-permute-start.14 = (f32[32,128]{1,0:T(8,128)S(1)}, f32[32,128]{1,0:T(8,128)S(1)}, u32[]{:S(2)}, u32[]{:S(2)}) collective-permute-start(f32[32,128]{1,0:T(8,128)S(1)} %add.49.refs_6_.refs_4_), channel_id=1, source_target_pairs={{0,96},{4,100},{8,104},{12,108},{16,112},{20,116},{24,120},{28,124... | collective-permute-start | bytes 49160 | tf_op jit(solution)/shard_map/ppermute | solution.py:355
  48.4 3.9 %collective-permute-start.16 = (f32[16,128]{1,0:T(8,128)S(1)}, f32[16,128]{1,0:T(8,128)S(1)}, u32[]{:S(2)}, u32[]{:S(2)}) collective-permute-start(f32[16,128]{1,0:T(8,128)S(1)} %pad_maximum_fusion), channel_id=1, source_target_pairs={{0,2},{1,3},{2,0},{3,1},{4,6},{5,7},{6,4},{7,5},{8,10},{9,11},{10,... | collective-permute-start | bytes 24584 | tf_op jit(solution)/shard_map/ppermute | solution.py:352
  54.5 3.9 %collective-permute-start.18 = (f32[56,128]{1,0:T(8,128)S(1)}, f32[56,128]{1,0:T(8,128)S(1)}, u32[]{:S(2)}, u32[]{:S(2)}) collective-permute-start(f32[56,128]{1,0:T(8,128)S(1)} %add.56), channel_id=1, source_target_pairs={{0,2},{1,3},{2,0},{3,1},{4,6},{5,7},{6,4},{7,5},{8,10},{9,11},{10,... | collective-permute-start | bytes 86024 | tf_op jit(solution)/shard_map/ppermute | solution.py:352
  58.4 5.1 %collective-permute-start.19 = (f32[56,128]{1,0:T(8,128)S(1)}, f32[56,128]{1,0:T(8,128)S(1)}, u32[]{:S(2)}, u32[]{:S(2)}) collective-permute-start(f32[56,128]{1,0:T(8,128)S(1)} %add.57.refs_0_), channel_id=1, source_target_pairs={{0,18},{1,19},{2,16},{3,17},{4,22},{5,23},{6,20},{7,21},{8,26},{9,... | collective-permute-start | bytes 86024 | tf_op jit(solution)/shard_map/ppermute | solution.py:512
  63.4 4.9 %collective-permute-start.22 = (f32[24,128]{1,0:T(8,128)S(1)}, f32[24,128]{1,0:T(8,128)S(1)}, u32[]{:S(2)}, u32[]{:S(2)}) collective-permute-start(f32[24,128]{1,0:T(8,128)S(1)} %shard_map.126), channel_id=1, source_target_pairs={{0,12},{4,8},{8,4},{12,0},{16,28},{20,24},{24,20},{28,16},{32,44},... | collective-permute-start | bytes 36872 | tf_op jit(solution)/shard_map/ppermute | solution.py:355
  65.5 5.2 %collective-permute-start.21 = (f32[24,128]{1,0:T(8,128)S(1)}, f32[24,128]{1,0:T(8,128)S(1)}, u32[]{:S(2)}, u32[]{:S(2)}) collective-permute-start(f32[24,128]{1,0:T(8,128)S(1)} %shard_map.126), channel_id=1, source_target_pairs={{0,8},{4,12},{8,0},{12,4},{16,24},{20,28},{24,16},{28,20},{32,40},... | collective-permute-start | bytes 36872 | tf_op jit(solution)/shard_map/ppermute | solution.py:355
  65.5 5.2 %collective-permute-start.20 = (f32[24,128]{1,0:T(8,128)S(1)}, f32[24,128]{1,0:T(8,128)S(1)}, u32[]{:S(2)}, u32[]{:S(2)}) collective-permute-start(f32[24,128]{1,0:T(8,128)S(1)} %shard_map.126), channel_id=1, source_target_pairs={{0,4},{4,0},{8,12},{12,8},{16,20},{20,16},{24,28},{28,24},{32,36},... | collective-permute-start | bytes 36872 | tf_op jit(solution)/shard_map/ppermute | solution.py:355
  70.7 5.0 %collective-permute-start.25 = (f32[24,128]{1,0:T(8,128)S(1)}, f32[24,128]{1,0:T(8,128)S(1)}, u32[]{:S(2)}, u32[]{:S(2)}) collective-permute-start(f32[24,128]{1,0:T(8,128)S(1)} %add_add_fusion.1), channel_id=1, source_target_pairs={{0,96},{4,100},{8,104},{12,108},{16,112},{20,116},{24,120},{28,124... | collective-permute-start | bytes 36872 | tf_op jit(solution)/shard_map/ppermute | solution.py:355
  70.8 5.3 %collective-permute-start.24 = (f32[24,128]{1,0:T(8,128)S(1)}, f32[24,128]{1,0:T(8,128)S(1)}, u32[]{:S(2)}, u32[]{:S(2)}) collective-permute-start(f32[24,128]{1,0:T(8,128)S(1)} %add_add_fusion.1), channel_id=1, source_target_pairs={{0,64},{4,68},{8,72},{12,76},{16,80},{20,84},{24,88},{28,92},{32,9... | collective-permute-start | bytes 36872 | tf_op jit(solution)/shard_map/ppermute | solution.py:355
  72.7 4.0 %collective-permute-start.23 = (f32[24,128]{1,0:T(8,128)S(1)}, f32[24,128]{1,0:T(8,128)S(1)}, u32[]{:S(2)}, u32[]{:S(2)}) collective-permute-start(f32[24,128]{1,0:T(8,128)S(1)} %add_add_fusion.1), channel_id=1, source_target_pairs={{0,32},{4,36},{8,40},{12,44},{16,48},{20,52},{24,56},{28,60},{32,0... | collective-permute-start | bytes 36872 | tf_op jit(solution)/shard_map/ppermute | solution.py:355
  (7 other events, 28.7 us)
